TPU v7x, 32 devices: a whole 2x2x4 slice. The times are simulated.
32 devices in a mesh: lat: 16 (over z, x, core), lon: 2 (over y).
Axes of the slice: x: 2, y: 2, z: 4, core: 2. Of those that a mesh axis runs over, the one named last changes fastest.
Arguments:
- tokens: bfloat16 [4, 96, 24, 512], P(None, 'lat', 'lon'), may hold values from -6 to 6
- w_qkv: bfloat16 [512, 1536], P('lon'), may hold values from -0.25 to 0.25
- w_out: bfloat16 [512, 512], P('lon'), may hold values from -0.25 to 0.25
- gain: float32 [512], replicated, may hold values from 0.1 to 1.9
- tau: float32 [8], replicated, may hold values from 1 to 12
- cotangent: bfloat16 [4, 96, 24, 512], P(None, 'lat', 'lon'), may hold values from -6 to 6
Outputs:
- output: bfloat16 [4, 96, 24, 512], P(None, 'lat', 'lon')
- grad_tokens: bfloat16 [4, 96, 24, 512], P(None, 'lat', 'lon')
- grad_qkv: float32 [512, 1536], P('lon')
- grad_out: float32 [512, 512], P('lon')
All inputs are finite; a program needn't handle non-finite values.
Results may differ from a plain program's by a relative error of at most 0.035.
Values may be sent and summed in bfloat16 or wider, within the bound.
A program may use at most 128 MiB of HBM per device.

v0:
```python
import jax
import jax.numpy as jnp
from jax import lax
from jax.sharding import PartitionSpec as P

LV = 4
WL = 2
WH = 6
WW = 12
KEYS = 288


NORM_EPS = 1e-05
UNIT_EPS = 1e-06


def with_halo(shard, sides, width, wrap):
    for axis, dim in sides:
        peers, length = (lax.axis_size(axis), shard.shape[dim])
        up = [(i, (i + 1) % peers) for i in range(peers if wrap else peers - 1)]
        down = [(j, i) for i, j in up]
        last = lax.slice_in_dim(shard, length - width, length, axis=dim)
        initial = lax.slice_in_dim(shard, 0, width, axis=dim)
        before = lax.ppermute(last, axis, up)
        after = lax.ppermute(initial, axis, down)
        shard = jnp.concatenate([before, shard, after], axis=dim)
    return shard


def from_behind(block, axis, distance):
    devices = range(lax.axis_size(axis))
    route = [((i - distance) % len(devices), i) for i in devices]
    return lax.ppermute(block, axis, route)


def from_behind_2(block, axis, distance):
    devices = range(lax.axis_size(axis))
    route = [(i - distance, i) for i in devices if i - distance in devices]
    return lax.ppermute(block, axis, route)


def unit_rows(vectors):
    scaling = lax.rsqrt(jnp.sum(vectors * vectors, axis=-1, keepdims=True) + UNIT_EPS)
    return (vectors * scaling, scaling)


def unit_back(vectors, scaling, gradient):
    inner_sum = jnp.sum(vectors * gradient, axis=-1, keepdims=True)
    return scaling * (gradient - vectors * (inner_sum * scaling * scaling))


def norm_forward(y_rows):
    centered = y_rows - jnp.mean(y_rows, axis=-1, keepdims=True)
    inverse = lax.rsqrt(jnp.mean(centered * centered, axis=-1, keepdims=True) + NORM_EPS)
    return (centered * inverse, inverse)


def norm_back(normed, inverse, upstream):
    mean_up = jnp.mean(upstream, axis=-1, keepdims=True)
    mean_cross = jnp.mean(upstream * normed, axis=-1, keepdims=True)
    return inverse * (upstream - mean_up - normed * mean_cross)


def key_windows(extended):
    ext_rows = extended.shape[1]
    ext_cols = extended.shape[2]
    channels = extended.shape[3]
    shaped = extended.reshape(LV, ext_rows // WH, WH, ext_cols // WW, WW, channels)
    return shaped.transpose(1, 3, 0, 2, 4, 5).reshape(
        ext_rows // WH, ext_cols // WW, KEYS, channels
    )


def key_layout(windows):
    win_rows = windows.shape[0]
    win_cols = windows.shape[1]
    channels = windows.shape[3]
    shaped = windows.reshape(win_rows, win_cols, LV, WH, WW, channels)
    return shaped.transpose(2, 0, 3, 1, 4, 5).reshape(LV, win_rows * WH, win_cols * WW, channels)


def query_units(own_grid):
    lat_rows = own_grid.shape[1]
    lon_cols = own_grid.shape[2]
    channels = own_grid.shape[3]
    half_h = WH // 2
    half_w = WW // 2
    shaped = own_grid.reshape(LV, lat_rows // half_h, half_h, lon_cols // half_w, half_w, channels)
    return shaped.transpose(1, 3, 0, 2, 4, 5).reshape(
        lat_rows // half_h, lon_cols // half_w, LV * half_h * half_w, channels
    )


def query_layout(units):
    row_units = units.shape[0]
    col_units = units.shape[1]
    channels = units.shape[3]
    half_h = WH // 2
    half_w = WW // 2
    shaped = units.reshape(row_units, col_units, LV, half_h, half_w, channels)
    return shaped.transpose(2, 0, 3, 1, 4, 5).reshape(
        LV, row_units * half_h, col_units * half_w, channels
    )


def spread_units(blocks, along):
    win_total = blocks.shape[along]
    first_part = lax.slice_in_dim(blocks, 0, 1, axis=along)
    middle_part = jnp.repeat(lax.slice_in_dim(blocks, 1, win_total - 1, axis=along), 2, axis=along)
    last_part = lax.slice_in_dim(blocks, win_total - 1, win_total, axis=along)
    return jnp.concatenate([first_part, middle_part, last_part], axis=along)


def merge_units(units, along):
    unit_total = units.shape[along]
    first_part = lax.slice_in_dim(units, 0, 1, axis=along)
    last_part = lax.slice_in_dim(units, unit_total - 1, unit_total, axis=along)
    middle = lax.slice_in_dim(units, 1, unit_total - 1, axis=along)
    new_shape = middle.shape[:along] + ((unit_total - 2) // 2, 2) + middle.shape[along + 1 :]
    middle_part = jnp.sum(middle.reshape(new_shape), axis=along + 1)
    return jnp.concatenate([first_part, middle_part, last_part], axis=along)


def cross_rows(left_mat, right_mat):
    return lax.dot_general(
        left_mat, right_mat, (((0,), (0,)), ((), ())), preferred_element_type=jnp.float32
    )


def on_device(tokens, w_qkv, w_out, gain, tau, cotangent):
    lat_rows = tokens.shape[1]
    lon_cols = tokens.shape[2]
    model_width = tokens.shape[3]
    head_count = tau.shape[0]
    head_dim = model_width // head_count
    tok_count = LV * lat_rows * lon_cols
    half_h = WH // 2
    half_w = WW // 2
    tok_flat = tokens.reshape(tok_count, model_width)
    src_count = tok_flat.shape[0]
    tok_part = tok_flat
    projected = jnp.dot(
        tok_part,
        lax.all_gather(w_qkv, "lon", axis=0, tiled=True),
        preferred_element_type=jnp.float32,
    )
    proj_b = projected.astype(jnp.bfloat16)
    query_grid = proj_b[:, :model_width].reshape(LV, lat_rows, lon_cols, model_width)
    query_f = query_grid.astype(jnp.float32).reshape(tok_count, head_count, head_dim)
    key_f = (
        proj_b[:, model_width : 2 * model_width]
        .astype(jnp.float32)
        .reshape(src_count, head_count, head_dim)
    )
    query_n, query_scale = unit_rows(query_f)
    key_n, key_scale = unit_rows(key_f)
    query_b = query_n.astype(jnp.bfloat16).reshape(LV, lat_rows, lon_cols, model_width)
    key_b = key_n.astype(jnp.bfloat16).reshape(src_count, model_width)
    kv_source = jnp.concatenate([key_b, proj_b[:, 2 * model_width :]], axis=1).reshape(
        LV, lat_rows, lon_cols, 2 * model_width
    )
    ext_rows = with_halo(kv_source, (("lat", 1),), half_h, False)
    ext_all = with_halo(ext_rows, (("lon", 2),), half_w, True)
    keys_units = spread_units(spread_units(key_windows(ext_all), 0), 1)
    row_units = keys_units.shape[0]
    col_units = keys_units.shape[1]
    key_u = keys_units[..., :model_width].reshape(row_units, col_units, KEYS, head_count, head_dim)
    value_u = keys_units[..., model_width:].reshape(
        row_units, col_units, KEYS, head_count, head_dim
    )
    query_count = LV * half_h * half_w
    query_u = query_units(query_b).reshape(row_units, col_units, query_count, head_count, head_dim)
    token_ids = jnp.arange(KEYS)
    query_ids = jnp.arange(query_count)
    key_level = (token_ids // (WH * WW) + WL // 2) // WL
    query_level = (query_ids // (half_h * half_w) + WL // 2) // WL
    same_level = query_level[:, None] == key_level[None, :]
    unit_ids = jnp.arange(row_units)
    ext_row = WH * ((unit_ids[:, None] + 1) // 2) + token_ids[None, :] // WW % WH
    global_row = lax.axis_index("lat") * lat_rows - half_h + ext_row
    inside = (global_row >= 0) & (global_row < lat_rows * lax.axis_size("lat"))
    allowed = (same_level[None, :, :] & inside[:, None, :]).astype(jnp.float32)[:, None, None]
    temper = tau[:, None, None]
    scores = (
        jnp.einsum("abqhd,abkhd->abhqk", query_u, key_u, preferred_element_type=jnp.float32)
        * temper
    )
    weights = jnp.exp(scores) * allowed
    probs = weights / jnp.sum(weights, axis=-1, keepdims=True)
    probs_b = probs.astype(jnp.bfloat16)
    mixed = jnp.einsum(
        "abhqk,abkhd->abqhd", probs_b, value_u, preferred_element_type=jnp.float32
    ).astype(jnp.bfloat16)
    attended = query_layout(mixed.reshape(row_units, col_units, query_count, model_width)).reshape(
        tok_count, model_width
    )
    att_part = attended
    y_rows = jnp.dot(
        att_part,
        lax.all_gather(w_out, "lon", axis=0, tiled=True),
        preferred_element_type=jnp.float32,
    )
    normed, inverse = norm_forward(y_rows)
    output = (tok_flat.astype(jnp.float32) + gain * normed).astype(jnp.bfloat16)
    cot_flat = cotangent.reshape(tok_count, model_width).astype(jnp.float32)
    grad_y = norm_back(normed, inverse, gain * cot_flat).astype(jnp.bfloat16)
    grad_att = jnp.dot(
        grad_y,
        lax.all_gather(w_out, "lon", axis=0, tiled=True).T,
        preferred_element_type=jnp.float32,
    )
    grad_att_b = grad_att.astype(jnp.bfloat16).reshape(LV, lat_rows, lon_cols, model_width)
    grad_u = query_units(grad_att_b).reshape(
        row_units, col_units, query_count, head_count, head_dim
    )
    dprob = jnp.einsum("abqhd,abkhd->abhqk", grad_u, value_u, preferred_element_type=jnp.float32)
    total_sum = jnp.sum(probs * dprob, axis=-1, keepdims=True)
    dscore = (temper * (probs * (dprob - total_sum))).astype(jnp.bfloat16)
    dquery = jnp.einsum("abhqk,abkhd->abqhd", dscore, key_u, preferred_element_type=jnp.float32)
    dkey = jnp.einsum("abhqk,abqhd->abkhd", dscore, query_u, preferred_element_type=jnp.float32)
    dvalue = jnp.einsum("abhqk,abqhd->abkhd", probs_b, grad_u, preferred_element_type=jnp.float32)
    key_grads = jnp.concatenate(
        [
            dkey.reshape(row_units, col_units, KEYS, model_width),
            dvalue.reshape(row_units, col_units, KEYS, model_width),
        ],
        axis=3,
    )
    ext_grad = key_layout(merge_units(merge_units(key_grads, 0), 1))
    dquery_own = query_layout(
        dquery.reshape(row_units, col_units, query_count, model_width)
    ).reshape(tok_count, head_count, head_dim)
    grad_q = unit_back(query_f, query_scale, dquery_own).reshape(
        LV, lat_rows, lon_cols, model_width
    )
    west_rim = ext_grad[:, :, :half_w]
    east_rim = ext_grad[:, :, half_w + lon_cols :]
    center = ext_grad[:, :, half_w : half_w + lon_cols]
    from_east = from_behind(west_rim.astype(jnp.bfloat16), "lon", -1).astype(west_rim.dtype)
    from_west = from_behind(east_rim.astype(jnp.bfloat16), "lon", 1).astype(east_rim.dtype)
    center = center.at[:, :, :half_w].add(from_west).at[:, :, lon_cols - half_w :].add(from_east)
    north_rim = center[:, :half_h]
    south_rim = center[:, half_h + lat_rows :]
    middle = center[:, half_h : half_h + lat_rows]
    from_south = from_behind_2(north_rim.astype(jnp.bfloat16), "lat", -1).astype(north_rim.dtype)
    from_north = from_behind_2(south_rim.astype(jnp.bfloat16), "lat", 1).astype(south_rim.dtype)
    middle = middle.at[:, :half_h].add(from_north).at[:, lat_rows - half_h :].add(from_south)
    own_grads = middle.reshape(tok_count, 2 * model_width)
    grad_k = unit_back(
        key_f, key_scale, own_grads[:, :model_width].reshape(tok_count, head_count, head_dim)
    ).reshape(tok_count, model_width)
    grad_q_src = grad_q.reshape(tok_count, model_width)
    dvalue_src = own_grads[:, model_width:]
    grad_proj = jnp.concatenate([grad_q_src, grad_k, dvalue_src], axis=1).astype(jnp.bfloat16)
    grad_in = jnp.dot(
        grad_proj,
        lax.all_gather(w_qkv, "lon", axis=0, tiled=True).T,
        preferred_element_type=jnp.float32,
    )
    grad_tokens = (
        (cot_flat + grad_in).astype(jnp.bfloat16).reshape(LV, lat_rows, lon_cols, model_width)
    )
    tok_part = tok_flat
    att_part = attended
    shard_sum = lax.psum_scatter(
        jnp.concatenate(
            [cross_rows(tok_part, grad_proj), cross_rows(att_part, grad_y)], axis=1
        ).astype(jnp.bfloat16),
        "lon",
        scatter_dimension=0,
        tiled=True,
    )
    summed = lax.psum(shard_sum, "lat").astype(jnp.float32)
    grad_qkv = summed[:, : 3 * model_width]
    grad_out = summed[:, 3 * model_width :]
    return (output.reshape(LV, lat_rows, lon_cols, model_width), grad_tokens, grad_qkv, grad_out)


def solution(mesh):
    in_specs = (
        P(None, "lat", "lon", None),
        P("lon", None),
        P("lon", None),
        P(),
        P(),
        P(None, "lat", "lon", None),
    )
    out_specs = (
        P(None, "lat", "lon", None),
        P(None, "lat", "lon", None),
        P("lon", None),
        P("lon", None),
    )
    return jax.shard_map(
        on_device, mesh=mesh, in_specs=in_specs, out_specs=out_specs, check_vma=False
    )
```

profile of v0, /device:TPU:1, one launch (start us, length us, event | category | flops | bytes accessed | tf_op | source)
XLA Modules:
  0.0 384.8 jit_solution(10404639011092765246)
XLA Ops:
  11.5 27.4 %all-gather.2.cloned.1.call-done = bf16[512,1536]{1,0:T(8,128)(2,1)} async-done(((bf16[256,1536]{1,0:T(8,128)(2,1)}), bf16[512,1536]{1,0:T(8,128)(2,1)}) %all-gather.2.cloned.1.call-update) | async-done | bytes 1572880 | tf_op jit(solution)/shard_map/all_gather | solution.py:144
  44.4 3.6 collective-permute-start
  50.0 7.6 %all_gather.9 = bf16[512,512]{1,0:T(8,128)(2,1)} all-gather(bf16[256,512]{1,0:T(8,128)(2,1)S(1)} %copy-done.31), channel_id=1, replica_groups=mesh['lat'=16,'lon'=2] {'lon'}, dimensions={0}, use_global_device_ids=true | all-gather | bytes 786432 | tf_op jit(solution)/shard_map/all_gather | solution.py:200
  72.2 7.1 %collective-permute-done.2 = bf16[4,12,6,1024]{3,0,2,1:T(4,128)(2,1)} collective-permute-done((bf16[4,12,6,1024]{3,0,2,1:T(4,128)(2,1)}, bf16[4,12,6,1024]{3,0,2,1:T(4,128)(2,1)}, u32[]{:S(2)}, u32[]{:S(2)}) %collective-permute-start.2) | collective-permute-done | bytes 589856 | tf_op jit(solution)/shard_map/ppermute | solution.py:24
  80.6 10.8 %collective-permute-done.3 = bf16[4,12,6,1024]{3,0,2,1:T(4,128)(2,1)} collective-permute-done((bf16[4,12,6,1024]{3,0,2,1:T(4,128)(2,1)}, bf16[4,12,6,1024]{3,0,2,1:T(4,128)(2,1)}, u32[]{:S(2)}, u32[]{:S(2)}) %collective-permute-start.3) | collective-permute-done | bytes 589856 | tf_op jit(solution)/shard_map/ppermute | solution.py:25
  100.3 3.2 pad_maximum_fusion.3
  103.5 2.8 copy.113
  106.3 4.3 %copy.109 = bf16[2,2,288,512]{2,3,1,0:T(8,128)(2,1)} copy(bf16[2,2,288,512]{3,1,2,0:T(2,128)(2,1)} %get-tuple-element.71) | data formatting | bytes 2359296 | tf_op jit(solution)/shard_map/slice | solution.py:168
  123.4 3.8 fusion.62
  127.2 2.8 convolution_bitcast_fusion
  130.0 16.7 %fusion.13 = f32[2,2,288,8,64]{2,4,3,1,0:T(8,128)} fusion(bf16[2,2,72,8,64]{2,4,3,1,0:T(8,128)(2,1)S(1)} %copy-done.18, f32[2,2,8,72,288]{4,3,2,1,0:T(8,128)} %fusion.62, f32[8]{0:T(128)S(1)} %copy-done.39, f32[2,2,8,72,288]{4,3,2,1,0:T(8,128)} %copy-done.13, f32[2,2,8,72]{3,2,1,0:T(8,128)S(1)} %get-tuple-element.86, f32[2,72,288]{2,1,0:T(8,128)S(1)} %copy-done.28), kind=kOutput, calls=%fused_computation.18 | convolution fusion | flops 92236320 | bytes 8137760 | tf_op jit(solution)/shard_map/abhqk,abqhd->abkhd/dot_general | solution.py:220
  146.7 5.5 %copy.129 = f32[2,2,288,8,64]{4,3,1,2,0:T(8,128)} copy(f32[2,2,288,8,64]{2,4,3,1,0:T(8,128)} %fusion.13) | data formatting | bytes 4718592 | tf_op jit(solution)/shard_map/abhqk,abqhd->abkhd/transpose | solution.py:220
  152.2 4.1 %concatenate.50 = f32[2,2,4,6,12,512]{5,1,4,3,2,0:T(2,128)S(1)} reshape(f32[2,2,288,8,64]{4,3,1,2,0:T(8,128)} %copy.129) | data formatting | bytes 4718592 | tf_op jit(solution)/shard_map/concatenate | solution.py:222
  156.3 5.5 %copy.131 = f32[2,2,288,8,64]{4,3,1,2,0:T(8,128)} copy(f32[2,2,288,8,64]{2,4,3,1,0:T(8,128)} %convolution_bitcast_fusion) | data formatting | bytes 4718592 | tf_op jit(solution)/shard_map/abhqk,abqhd->abkhd/transpose | solution.py:221
  161.9 5.7 %concatenate.51 = f32[2,2,4,6,12,512]{5,1,4,3,2,0:T(2,128)} reshape(f32[2,2,288,8,64]{4,3,1,2,0:T(8,128)} %copy.131) | data formatting | bytes 4718592 | tf_op jit(solution)/shard_map/concatenate | solution.py:222
  167.5 4.2 %maximum_bitcast_fusion = f32[4,2,6,2,12,1024]{5,3,4,2,0,1:T(2,128)S(1)} fusion(f32[2,2,4,6,12,512]{5,1,4,3,2,0:T(2,128)} %concatenate.51, f32[2,2,4,6,12,512]{5,1,4,3,2,0:T(2,128)S(1)} %concatenate.50), kind=kLoop, calls=%fused_computation.1 | loop fusion | flops 1179648 | bytes 9437184 | tf_op jit(solution)/shard_map/transpose | solution.py:79
  171.7 3.1 copy.132
  181.2 18.4 %fusion.18 = f32[2,2,72,8,64]{2,4,3,1,0:T(8,128)} fusion(bf16[2,2,288,8,64]{2,4,3,1,0:T(8,128)(2,1)S(1)} %bitcast.79, f32[2,2,8,72,288]{4,3,2,1,0:T(8,128)} %fusion.62, f32[8]{0:T(128)S(1)} %copy-done.39, f32[2,2,8,72,288]{4,3,2,1,0:T(8,128)} %copy-done.13, f32[2,2,8,72]{3,2,1,0:T(8,128)S(1)} %get-tuple-element.86, f32[2,72,288]{2,1,0:T(8,128)} %and_convert_fusion), kind=kOutput, calls=%fused_computation.22 | convolution fusion | flops 92236320 | bytes 7253024 | tf_op jit(solution)/shard_map/abhqk,abkhd->abqhd/dot_general | solution.py:219
  199.6 2.6 slice.241
  202.2 2.7 copy.122
  212.0 2.6 copy.125
  221.9 5.1 %collective-permute-start.6 = (bf16[4,3,12,1024]{3,0,2,1:T(4,128)(2,1)}, bf16[4,3,12,1024]{3,0,2,1:T(4,128)(2,1)}, u32[]{:S(2)}, u32[]{:S(2)}) collective-permute-start(bf16[4,3,12,1024]{3,0,2,1:T(4,128)(2,1)} %get-tuple-element.77), channel_id=1, source_target_pairs={{0,2},{2,4},{4,6},{6,8},{8,10},{10,12},{12,14},{14,16},{16,18},{18... | collective-permute-start | bytes 884744 | tf_op jit(solution)/shard_map/ppermute | solution.py:39
  247.3 30.4 %reduce-scatter.2.cloned.1.call-done = bf16[256,2048]{0,1:T(8,128)(2,1)} async-done(((bf16[512,2048]{0,1:T(8,128)(2,1)}), bf16[256,2048]{0,1:T(8,128)(2,1)}) %reduce-scatter.2.cloned.1.call-update) | async-done | bytes 1048592 | tf_op jit(solution)/shard_map/reduce_scatter | solution.py:265
  281.9 92.3 %all-reduce.2.cloned.1.call-done = bf16[256,2048]{0,1:T(8,128)(2,1)} async-done(((bf16[256,2048]{0,1:T(8,128)(2,1)}), bf16[256,2048]{0,1:T(8,128)(2,1)}) %all-reduce.2.cloned.1.call-update) | async-done | bytes 1048592 | tf_op jit(solution)/shard_map/psum | solution.py:273
  (208 shorter events, 97.7 us)
Async XLA Ops:
  7.2 31.7 %all-gather.2.cloned.1.call-start = ((), (), s32[]{:S(2)}) async-start(), calls=%async_computation.1 | async-start | bytes 2359296 | tf_op jit(solution)/shard_map/all_gather | solution.py:144
  7.9 269.8 %reduce-scatter.2.cloned.1.call-start = ((), (), s32[]{:S(2)}) async-start(), calls=%async_computation.2 | async-start | bytes 3145728 | tf_op jit(solution)/shard_map/reduce_scatter | solution.py:265
  9.1 31.8 %copy-start.21 = (bf16[288,512]{1,0:T(8,128)(2,1)}, bf16[288,512]{1,0:T(8,128)(2,1)S(1)}, u32[]{:S(2)}) copy-start(bf16[288,512]{1,0:T(8,128)(2,1)S(1)} %reshape.455) | copy-start | bytes 884740
  43.2 6.8 %copy-start.31 = (bf16[256,512]{1,0:T(8,128)(2,1)S(1)}, bf16[256,512]{1,0:T(8,128)(2,1)}, u32[]{:S(2)}) copy-start(bf16[256,512]{1,0:T(8,128)(2,1)} %param.16) | copy-start | bytes 786436
  43.2 14.3 %copy-start.26 = (bf16[4,6,12,512]{3,0,2,1:T(4,128)(2,1)S(1)}, bf16[4,6,12,512]{3,0,2,1:T(4,128)(2,1)}, u32[]{:S(2)}) copy-start(bf16[4,6,12,512]{3,0,2,1:T(4,128)(2,1)} %param.19) | copy-start | bytes 884740
  43.4 15.1 %copy-start.32 = (f32[4,6,12]{0,2,1:T(8,128)S(1)}, f32[4,6,12]{0,2,1:T(8,128)}, u32[]{:S(2)}) copy-start(f32[4,6,12]{0,2,1:T(8,128)} %broadcast_multiply_fusion) | copy-start | bytes 3460
  43.4 15.4 %copy-start.33 = (pred[72,288]{1,0:T(8,128)(4,1)S(1)}, pred[72,288]{1,0:T(8,128)(4,1)}, u32[]{:S(2)}) copy-start(pred[72,288]{1,0:T(8,128)(4,1)} %broadcast_compare_fusion) | copy-start | bytes 62212
  44.4 16.4 %collective-permute-start = (bf16[4,3,12,1024]{3,2,1,0:T(8,128)(2,1)}, bf16[4,3,12,1024]{3,2,1,0:T(8,128)(2,1)S(1)}, u32[]{:S(2)}, u32[]{:S(2)}) collective-permute-start(bf16[4,3,12,1024]{3,2,1,0:T(8,128)(2,1)} %get-tuple-element.82), channel_id=1, source_target_pairs={{0,2},{2,4},{4,6},{6,8},{8,10},{10,12},{12,14},{14,16},{16,18},{18... | collective-permute-start | bytes 884744 | tf_op jit(solution)/shard_map/ppermute | solution.py:24
  48.0 12.7 %collective-permute-start.1 = (bf16[4,3,12,1024]{3,2,1,0:T(8,128)(2,1)}, bf16[4,3,12,1024]{3,2,1,0:T(8,128)(2,1)}, u32[]{:S(2)}, u32[]{:S(2)}) collective-permute-start(bf16[4,3,12,1024]{3,2,1,0:T(8,128)(2,1)} %get-tuple-element.83), channel_id=1, source_target_pairs={{2,0},{4,2},{6,4},{8,6},{10,8},{12,10},{14,12},{16,14},{18,16},{20... | collective-permute-start | bytes 884744 | tf_op jit(solution)/shard_map/ppermute | solution.py:25
  63.7 15.7 %collective-permute-start.2 = (bf16[4,12,6,1024]{3,0,2,1:T(4,128)(2,1)}, bf16[4,12,6,1024]{3,0,2,1:T(4,128)(2,1)}, u32[]{:S(2)}, u32[]{:S(2)}) collective-permute-start(bf16[4,12,6,1024]{3,0,2,1:T(4,128)(2,1)} %copy.102), channel_id=1, source_target_pairs={{0,1},{1,0},{2,3},{3,2},{4,5},{5,4},{6,7},{7,6},{8,9},{9,8},{10,11... | collective-permute-start | bytes 1769480 | tf_op jit(solution)/shard_map/ppermute | solution.py:24
  65.2 26.3 %collective-permute-start.3 = (bf16[4,12,6,1024]{3,0,2,1:T(4,128)(2,1)}, bf16[4,12,6,1024]{3,0,2,1:T(4,128)(2,1)}, u32[]{:S(2)}, u32[]{:S(2)}) collective-permute-start(bf16[4,12,6,1024]{3,0,2,1:T(4,128)(2,1)} %copy.103), channel_id=1, source_target_pairs={{1,0},{0,1},{3,2},{2,3},{5,4},{4,5},{7,6},{6,7},{9,8},{8,9},{11,10... | collective-permute-start | bytes 1769480 | tf_op jit(solution)/shard_map/ppermute | solution.py:25
  103.5 7.1 %copy-start.17 = (bf16[2,2,72,8,64]{2,4,3,1,0:T(8,128)(2,1)S(1)}, bf16[2,2,72,8,64]{2,4,3,1,0:T(8,128)(2,1)}, u32[]{:S(2)}) copy-start(bf16[2,2,72,8,64]{2,4,3,1,0:T(8,128)(2,1)} %copy.114) | copy-start | bytes 884740
  103.5 7.1 %copy-start.27 = (f32[2,72,288]{2,1,0:T(8,128)S(1)}, f32[2,72,288]{2,1,0:T(8,128)}, u32[]{:S(2)}) copy-start(f32[2,72,288]{2,1,0:T(8,128)} %and_convert_fusion) | copy-start | bytes 497668
  103.5 7.1 %copy-start.39 = (f32[8]{0:T(128)S(1)}, f32[8]{0:T(128)}, u32[]{:S(2)}) copy-start(f32[8]{0:T(128)} %param.18) | copy-start | bytes 100
  178.6 38.2 %collective-permute-start.4 = (bf16[4,12,6,1024]{3,0,2,1:T(4,128)(2,1)}, bf16[4,12,6,1024]{3,0,2,1:T(4,128)(2,1)}, u32[]{:S(2)}, u32[]{:S(2)}) collective-permute-start(bf16[4,12,6,1024]{3,0,2,1:T(4,128)(2,1)} %get-tuple-element.69), channel_id=1, source_target_pairs={{1,0},{0,1},{3,2},{2,3},{5,4},{4,5},{7,6},{6,7},{9,8},{8,9},{11,10... | collective-permute-start | bytes 1769480 | tf_op jit(solution)/shard_map/ppermute | solution.py:33
  179.8 38.9 %collective-permute-start.5 = (bf16[4,12,6,1024]{3,0,2,1:T(4,128)(2,1)}, bf16[4,12,6,1024]{3,0,2,1:T(4,128)(2,1)}, u32[]{:S(2)}, u32[]{:S(2)}) collective-permute-start(bf16[4,12,6,1024]{3,0,2,1:T(4,128)(2,1)} %get-tuple-element.68), channel_id=1, source_target_pairs={{1,0},{0,1},{3,2},{2,3},{5,4},{4,5},{7,6},{6,7},{9,8},{8,9},{11,10... | collective-permute-start | bytes 1769480 | tf_op jit(solution)/shard_map/ppermute | solution.py:33
  220.3 6.6 %copy-start.15 = (f32[288,8,64]{0,2,1:T(8,128)S(1)}, f32[288,8,64]{0,2,1:T(8,128)}, u32[]{:S(2)}) copy-start(f32[288,8,64]{0,2,1:T(8,128)} %copy.125) | copy-start | bytes 1769476
  220.4 8.7 %copy-start.37 = (f32[288,8]{0,1:T(8,128)S(1)}, f32[288,8]{0,1:T(8,128)}, u32[]{:S(2)}) copy-start(f32[288,8]{0,1:T(8,128)} %copy-done.36) | copy-start | bytes 27652
  221.9 10.5 %collective-permute-start.6 = (bf16[4,3,12,1024]{3,0,2,1:T(4,128)(2,1)}, bf16[4,3,12,1024]{3,0,2,1:T(4,128)(2,1)}, u32[]{:S(2)}, u32[]{:S(2)}) collective-permute-start(bf16[4,3,12,1024]{3,0,2,1:T(4,128)(2,1)} %get-tuple-element.77), channel_id=1, source_target_pairs={{0,2},{2,4},{4,6},{6,8},{8,10},{10,12},{12,14},{14,16},{16,18},{18... | collective-permute-start | bytes 884744 | tf_op jit(solution)/shard_map/ppermute | solution.py:39
  227.1 8.1 %collective-permute-start.7 = (bf16[4,3,12,1024]{3,0,2,1:T(4,128)(2,1)S(1)}, bf16[4,3,12,1024]{3,0,2,1:T(4,128)(2,1)}, u32[]{:S(2)}, u32[]{:S(2)}) collective-permute-start(bf16[4,3,12,1024]{3,0,2,1:T(4,128)(2,1)S(1)} %get-tuple-element.76), channel_id=1, source_target_pairs={{2,0},{4,2},{6,4},{8,6},{10,8},{12,10},{14,12},{16,14},{18,16},{20... | collective-permute-start | bytes 884744 | tf_op jit(solution)/shard_map/ppermute | solution.py:39
  247.2 30.5 %copy-start.24 = (bf16[288,512]{1,0:T(8,128)(2,1)S(1)}, bf16[288,512]{1,0:T(8,128)(2,1)}, u32[]{:S(2)}) copy-start(bf16[288,512]{1,0:T(8,128)(2,1)} %get-tuple-element.85) | copy-start | bytes 884740
  247.2 31.6 %copy-start.8 = (f32[288,512]{1,0:T(8,128)S(1)}, f32[288,512]{1,0:T(8,128)}, u32[]{:S(2)}) copy-start(f32[288,512]{1,0:T(8,128)} %reshape.465) | copy-start | bytes 1769476
  247.2 31.6 %copy-start.30 = (bf16[288,512]{1,0:T(8,128)(2,1)S(1)}, bf16[288,512]{1,0:T(8,128)(2,1)}, u32[]{:S(2)}) copy-start(bf16[288,512]{1,0:T(8,128)(2,1)} %slice.283) | copy-start | bytes 884740
  247.2 126.9 %all-reduce.2.cloned.1.call-start = ((), (), s32[]{:S(2)}) async-start(), calls=%async_computation.3 | async-start | bytes 2097152 | tf_op jit(solution)/shard_map/psum | solution.py:273
  (27 other events, 65.3 us)
Sparse Core Ops, SparseCore 0:
  9.6 29.2 all-gather.1
  247.4 30.2 reduce-scatter.1
  281.6 92.5 all-reduce.1
where the time goes:
time: 390 us; the launch traced here: 385 us
  waiting for transfers between devices  170 us (44%)
  local copies, waits for them, and re-layouts  92.8 us (24%)
  matrix products  52.7 us (14%)
  other arithmetic  30.7 us (8%)
  starting transfers between devices  15.6 us (4%)
  between operations  14.9 us (4%)
  blocking collectives  7.6 us (2%)
    psum x1, waiting for transfers between devices, on_device(): summed = lax.psum(shard_sum, 'lat').astype(jnp.float32)  92.3 us
    reduce_scatter x1, waiting for transfers between devices, on_device(): lax.psum_scatter(jnp.concatenate([cross_rows(tok_part, grad_proj), cross_...  30.4 us
    all_gather x1, waiting for transfers between devices, on_device(): lax.all_gather(w_qkv, 'lon', axis=0, tiled=True)  27.4 us
    dot_general x1, matrix products, on_device(): jnp.einsum('abhqk,abkhd->abqhd', dscore, key_u, preferred_element_type=jn...  18.4 us
    dot_general x1, matrix products, on_device(): jnp.einsum('abhqk,abqhd->abkhd', dscore, query_u, preferred_element_type=...  16.7 us
    ppermute x2, waiting for transfers between devices, with_halo(): after = lax.ppermute(initial, axis, down)  10.8 us
    unnamed x87, local copies, waits for them, and re-layouts  10.6 us
    concatenate x2, local copies, waits for them, and re-layouts, on_device(): jnp.concatenate([dkey.reshape(row_units, col_units, KEYS, model_width), d...  9.78 us
  transfers between devices with their start and end apart: 11, of which 6 were waited for; matrix products, arithmetic and copies ran while one was open for 16% of the time, Pallas kernels for 0%

commit v1 on v0

v1 whole, which is shorter than its diff:
```python
import functools

import jax
import jax.numpy as jnp
from jax import lax
from jax.experimental import pallas as pl
from jax.experimental.pallas import tpu as pltpu
from jax.sharding import PartitionSpec as P

LV = 4
WH = 6
WW = 12
NORM_EPS = 1e-05
UNIT_EPS = 1e-06
MESH = pl.DeviceIdType.MESH
BF = jnp.bfloat16
F32 = jnp.float32
LEVELS = (0, 3, 1, 2)


def dot(a, b, ca, cb):
    return lax.dot_general(a, b, (((ca,), (cb,)), ((), ())), preferred_element_type=F32)


def bits_of(n):
    return n.bit_length() - 1


def norm_forward(y_rows):
    centered = y_rows - jnp.mean(y_rows, axis=-1, keepdims=True)
    inverse = lax.rsqrt(jnp.mean(centered * centered, axis=-1, keepdims=True) + NORM_EPS)
    return centered * inverse, inverse


def norm_back(normed, inverse, upstream):
    mean_up = jnp.mean(upstream, axis=-1, keepdims=True)
    mean_cross = jnp.mean(upstream * normed, axis=-1, keepdims=True)
    return inverse * (upstream - mean_up - normed * mean_cross)


class Copies:
    def __init__(self, send, recv):
        self.send, self.recv, self.used = send, recv, 0

    def make(self, src, dst, device):
        n = self.used
        self.used += 1
        return pltpu.make_async_remote_copy(
            src_ref=src, dst_ref=dst, send_sem=self.send.at[n], recv_sem=self.recv.at[n],
            device_id=device, device_id_type=MESH,
        )


def kernel(nlat, nlon, x_ref, wq_ref, wo_ref, gain_ref, tau_ref, home_ref, g_ref,
           xq, w, tok, proj, qn, kn, probs, att, dy, da, dqkv, oq, oq_in,
           f0, f1, r0, r1, a0, a1, send, recv):
    lat, lon = lax.axis_index("lat"), lax.axis_index("lon")
    D = 512
    R = D // nlon
    H = R // 2
    core = lat % 2
    sibling = lat + 1 - 2 * core

    def flip(index, bit):
        v = (index // (1 << bit)) % 2
        return index + (1 - 2 * v) * (1 << bit), v

    def ahead(a, b):
        return ((lat + a) % nlat, (lon + b) % nlon)

    def behind(a, b):
        return ((lat + nlat - a) % nlat, (lon + nlon - b) % nlon)

    moves = ((0, 1), (1, 0), (1, 1))
    peers = [ahead(a, b) for a, b in moves] + [behind(a, b) for a, b in moves]
    peers += [(lat, (lon + d) % nlon) for d in range(1, nlon)]
    peers += [(flip(lat, b)[0], lon) for b in range(bits_of(nlat))]
    barrier = pltpu.get_barrier_semaphore()
    for device in peers:
        pl.semaphore_signal(barrier, inc=1, device_id=device, device_id_type=MESH)
    pl.semaphore_wait(barrier, len(peers))

    copies = Copies(send, recv)
    waits = []

    def w_source(p):
        if p < 3:
            return wq_ref.at[pl.ds(core * H, H), pl.ds(p * D, D)]
        return wo_ref.at[pl.ds(core * H, H), :]

    halo = []
    for a, b in moves:
        c = copies.make(x_ref.at[2 * a + b], xq.at[2 * (1 - a) + 1 - b], ahead(a, b))
        c.start()
        halo.append(c)
    across, forward = [], []
    for p in range(4):
        across.append([])
        for d in range(1, nlon):
            c = copies.make(w_source(p), w.at[p, pl.ds(lon * R + core * H, H), :],
                            (lat, (lon + d) % nlon))
            c.start()
            across[p].append(c)
    for p in range(4):
        row = []
        for d in range(1, nlon):
            first = ((lon + nlon - d) % nlon) * R + core * H
            part = w.at[p, pl.ds(first, H), :]
            row.append(copies.make(part, part, (sibling, lon)))
        forward.append(row)

    xq[3] = x_ref[0]
    for p in range(3):
        w[p, pl.ds(lon * R, R), :] = wq_ref[:, p * D:(p + 1) * D]
    w[3, pl.ds(lon * R, R), :] = wo_ref[...]

    for c in halo:
        c.wait_recv()
    to = lax.broadcasted_iota(jnp.int32, (288, 576), 0)
    src = lax.broadcasted_iota(jnp.int32, (288, 576), 1)
    want = ((to % 144) // 36) * 144 + (to // 144) * 36 + to % 36
    flat = xq[...].reshape(576, D)
    tokens = dot((want == src).astype(BF), flat, 1, 0).astype(BF)
    cot = dot((want + 72 == src).astype(BF), flat, 1, 0)
    tok[...] = tokens

    def arrive(p):
        for c in across[p]:
            c.wait_recv()
        for c in forward[p]:
            c.start()

    def project(p):
        for c in forward[p]:
            c.wait_recv()
        proj[p] = dot(tok[...], w[p], 1, 0).astype(BF)

    arrive(0)
    arrive(1)
    project(0)
    arrive(2)
    project(1)
    arrive(3)
    project(2)

    kk = lax.broadcasted_iota(jnp.int32, (144, 144), 0)
    qq = lax.broadcasted_iota(jnp.int32, (144, 144), 1)
    rows_ok = ((kk // 72) == (qq // 72)) | (jnp.zeros_like(kk) + lat != 0)
    level_ok = ((kk % 36) // 18) == ((qq % 36) // 18)

    def place(step):
        g, pair = step // 4, step % 4
        return (g, pair, pl.ds(pl.multiple_of(g * 144, 16), 144),
                pl.ds(pl.multiple_of(pair * 128, 128), 128))

    def halves(x):
        return x[:, :64], x[:, 64:]

    def unit(x):
        x = x.astype(F32)
        return (x * lax.rsqrt(jnp.sum(x * x, axis=-1, keepdims=True) + UNIT_EPS)).astype(BF)

    def forward_step(step, carry):
        g, pair, rs, cs = place(step)
        qs = [unit(x) for x in halves(proj[0, rs, cs])]
        ks = [unit(x) for x in halves(proj[1, rs, cs])]
        qn[rs, cs] = jnp.concatenate(qs, axis=1)
        kn[rs, cs] = jnp.concatenate(ks, axis=1)
        vs = halves(proj[2, rs, cs])
        mask = (rows_ok & (level_ok | (jnp.zeros_like(kk) + g == 1))).astype(F32)
        outs = []
        for i in range(2):
            s = dot(ks[i], qs[i], 1, 1) * tau_ref[2 * pair + i]
            e = jnp.exp(s) * mask
            p = e * (1.0 / jnp.sum(e, axis=0, keepdims=True))
            probs[2 * step + i] = p
            outs.append(dot(p.astype(BF), vs[i], 0, 0))
        att[rs, cs] = jnp.concatenate(outs, axis=1).astype(BF)
        return carry

    lax.fori_loop(0, 8, forward_step, 0)

    for c in forward[3]:
        c.wait_recv()
    normed, inverse = norm_forward(dot(att[...], w[3], 1, 0))
    gain = gain_ref[...]
    output = (tok[...].astype(F32) + gain * normed).astype(BF)
    dy[...] = norm_back(normed, inverse, gain * cot).astype(BF)
    da[...] = dot(dy[...], w[3], 1, 1).astype(BF)

    def dv_step(step, carry):
        g, pair, rs, cs = place(step)
        das = halves(da[rs, cs])
        dqkv[2, rs, cs] = jnp.concatenate(
            [dot(probs[2 * step + i].astype(BF), das[i], 1, 0) for i in range(2)], axis=1
        ).astype(BF)
        return carry

    lax.fori_loop(0, 8, dv_step, 0)

    half = 4 * D

    def place_gradient(f, which, grad, lon_first):
        for b in range(nlon):
            for ch in range(4):
                if lon_first:
                    first = which * half + b * 4 * R + ch * R
                else:
                    first = which * half + (ch // 2) * (half // 2) + b * 2 * R + (ch % 2) * R
                f[first:first + R, :] = grad[b * R:(b + 1) * R, ch * 128:(ch + 1) * 128]

    lat_bits = [("lat", b) for b in range(bits_of(nlat))]
    lon_bits = [("lon", b) for b in reversed(range(bits_of(nlon)))]

    class Stream:
        def __init__(self, f, r, a, order):
            self.f, self.r, self.a, self.order = f, r, a, order
            self.stage, self.size, self.off = 0, 2 * half, 0
            self.gsize, self.goff = 2 * half // nlon, 0
            self.done, self.gathers = [], []

        def start(self):
            axis, bit = self.order[self.stage]
            self.size //= 2
            peer, mine = flip(lat if axis == "lat" else lon, bit)
            device = (peer, lon) if axis == "lat" else (lat, peer)
            self.base = 4 * half - 4 * self.size if False else 2 * half - 2 * self.size
            give = pl.multiple_of(self.off + (1 - mine) * self.size, 16)
            self.off = self.off + mine * self.size
            if axis == "lat":
                self.gsize //= 2
                self.gathers.append((device, self.gsize))
                self.goff = self.goff + mine * self.gsize
                self.gathers[-1] = (device, self.gsize, self.goff)
            self.copy = copies.make(self.f.at[pl.ds(give, self.size), :],
                                    self.r.at[pl.ds(self.base, self.size), :], device)
            self.copy.start()

        def finish(self):
            self.copy.wait_recv()
            self.done.append(self.copy)
            keep = pl.ds(pl.multiple_of(self.off, 16), self.size)
            total = (self.f[keep, :].astype(F32)
                     + self.r[self.base:self.base + self.size, :].astype(F32)).astype(BF)
            self.stage += 1
            if self.stage == len(self.order):
                self.a[pl.ds(pl.multiple_of(self.goff, 16), self.size), :] = total
            else:
                self.f[keep, :] = total

        def gather_start(self):
            device, size, off = self.gathers.pop()
            part = self.a.at[pl.ds(pl.multiple_of(off, 16), size), :]
            self.copy = copies.make(part, part, device)
            self.copy.start()

        def gather_finish(self):
            self.copy.wait_recv()
            self.done.append(self.copy)

    s0 = Stream(f0, r0, a0, lat_bits[:1] + lon_bits + lat_bits[1:])
    s1 = Stream(f1, r1, a1, lat_bits[:2] + lon_bits + lat_bits[2:])

    place_gradient(f0, 0, dot(att[...], dy[...], 0, 0).astype(BF), True)
    place_gradient(f0, 1, dot(tok[...], dqkv[2], 0, 0).astype(BF), True)
    s0.start()

    def back(x, n, grad):
        x = x.astype(F32)
        scale = lax.rsqrt(jnp.sum(x * x, axis=-1, keepdims=True) + UNIT_EPS)
        inner = jnp.sum(x * grad, axis=-1, keepdims=True)
        return scale * (grad - x * (inner * scale * scale))

    def ds_step(step, carry):
        g, pair, rs, cs = place(step)
        das, vs = halves(da[rs, cs]), halves(proj[2, rs, cs])
        qs, ks = halves(proj[0, rs, cs]), halves(proj[1, rs, cs])
        qns, kns = halves(qn[rs, cs]), halves(kn[rs, cs])
        dqs, dks = [], []
        for i in range(2):
            p = probs[2 * step + i]
            dp = dot(vs[i], das[i], 1, 1)
            tot = jnp.sum(p * dp, axis=0, keepdims=True)
            ds = (tau_ref[2 * pair + i] * (p * (dp - tot))).astype(BF)
            dqs.append(back(qs[i], qns[i], dot(ds, kns[i], 0, 0)))
            dks.append(back(ks[i], kns[i], dot(ds, qns[i], 1, 0)))
        dqkv[0, rs, cs] = jnp.concatenate(dqs, axis=1).astype(BF)
        dqkv[1, rs, cs] = jnp.concatenate(dks, axis=1).astype(BF)
        return carry

    lax.fori_loop(0, 8, ds_step, 0)

    s0.finish()
    s0.start()
    place_gradient(f1, 0, dot(tok[...], dqkv[0], 0, 0).astype(BF), False)
    place_gradient(f1, 1, dot(tok[...], dqkv[1], 0, 0).astype(BF), False)
    s1.start()

    grad_in = dot(dqkv[0], w[0], 1, 1) + dot(dqkv[1], w[1], 1, 1) + dot(dqkv[2], w[2], 1, 1)
    grad_tok = (cot + grad_in).astype(BF)
    to2 = lax.broadcasted_iota(jnp.int32, (576, 288), 0)
    src2 = lax.broadcasted_iota(jnp.int32, (576, 288), 1)
    inner = to2 % 144
    want2 = ((inner % 72) // 36) * 144 + (to2 // 144) * 36 + inner % 36
    first = ((want2 == src2) & (inner < 72)).astype(BF)
    second = ((want2 == src2) & (inner >= 72)).astype(BF)
    oq[...] = (dot(first, output, 1, 0) + dot(second, grad_tok, 1, 0)).astype(BF).reshape(4, 144, D)
    s1.finish()
    s1.start()
    homes = []
    for a, b in moves:
        c = copies.make(oq.at[2 * (1 - a) + 1 - b], oq_in.at[2 * a + b - 1], behind(a, b))
        c.start()
        homes.append(c)
    home_ref[0] = oq[3]

    total = len(s0.order)
    while s1.stage < total:
        if s0.stage < total:
            s0.finish()
            if s0.stage < total:
                s0.start()
            else:
                s0.gather_start()
        s1.finish()
        if s1.stage < total:
            s1.start()
    s1.gather_start()
    while True:
        s0.gather_finish()
        if s0.gathers:
            s0.gather_start()
        s1.gather_finish()
        if not s1.gathers:
            break
        s1.gather_start()
    if len(s0.gathers) > 0:
        raise ValueError

    for which, (a, p) in enumerate(((a0, 3), (a0, 2), (a1, 0), (a1, 1))):
        for ch in range(4):
            first = (which % 2) * (half // nlon) + ch * R
            g_ref[:, p * D + ch * 128:p * D + (ch + 1) * 128] = a[first:first + R, :]
    for i, c in enumerate(homes):
        c.wait_recv()
        home_ref[i + 1] = oq_in[i]
    for c in halo + homes + sum(across, []) + sum(forward, []) + s0.done + s1.done:
        c.wait_send()


def on_device(nlat, nlon, tokens, w_qkv, w_out, gain, tau, cotangent):
    D = tokens.shape[3]

    def quarters(x):
        x = jnp.stack([x[l] for l in LEVELS])
        x = x.reshape(LV, 2, WH // 2, 2, WW // 2, D).transpose(1, 3, 0, 2, 4, 5)
        return x.reshape(4, 72, D)

    x = jnp.concatenate([quarters(tokens), quarters(cotangent)], axis=1)
    R = D // nlon
    half = 4 * D
    n_copies = 6 + 8 * (nlon - 1) + 2 * (2 * bits_of(nlat) + bits_of(nlon))
    vm = pl.BlockSpec(memory_space=pltpu.VMEM)
    home, grads = pl.pallas_call(
        functools.partial(kernel, nlat, nlon),
        out_shape=(
            jax.ShapeDtypeStruct((4, 144, D), BF),
            jax.ShapeDtypeStruct((R, 4 * D), BF),
        ),
        in_specs=[vm] * 4 + [pl.BlockSpec(memory_space=pltpu.SMEM)],
        out_specs=(vm, vm),
        scratch_shapes=[
            pltpu.VMEM((4, 144, D), BF),
            pltpu.VMEM((4, D, D), BF),
            pltpu.VMEM((288, D), BF),
            pltpu.VMEM((3, 288, D), BF),
            pltpu.VMEM((288, D), BF),
            pltpu.VMEM((288, D), BF),
            pltpu.VMEM((16, 144, 144), F32),
            pltpu.VMEM((288, D), BF),
            pltpu.VMEM((288, D), BF),
            pltpu.VMEM((288, D), BF),
            pltpu.VMEM((3, 288, D), BF),
            pltpu.VMEM((4, 144, D), BF),
            pltpu.VMEM((3, 144, D), BF),
            pltpu.VMEM((2 * half, 128), BF),
            pltpu.VMEM((2 * half, 128), BF),
            pltpu.VMEM((2 * half, 128), BF),
            pltpu.VMEM((2 * half, 128), BF),
            pltpu.VMEM((2 * half // nlon, 128), BF),
            pltpu.VMEM((2 * half // nlon, 128), BF),
            pltpu.SemaphoreType.DMA((n_copies,)),
            pltpu.SemaphoreType.DMA((n_copies,)),
        ],
        compiler_params=pltpu.CompilerParams(
            collective_id=0, has_side_effects=True, vmem_limit_bytes=48 * 1024 * 1024
        ),
    )(x, w_qkv, w_out, gain.reshape(1, D), tau)

    def grid(q):
        q = q.reshape(2, 2, LV, WH // 2, WW // 2, D).transpose(2, 0, 3, 1, 4, 5)
        q = q.reshape(LV, WH, WW, D)
        return jnp.stack([q[LEVELS.index(l)] for l in range(LV)])

    return (
        grid(home[:, :72]),
        grid(home[:, 72:]),
        grads[:, : 3 * D].astype(F32),
        grads[:, 3 * D :].astype(F32),
    )


def solution(mesh):
    nlat, nlon = mesh.shape["lat"], mesh.shape["lon"]
    grid = P(None, "lat", "lon", None)
    rows = P("lon", None)
    return jax.shard_map(
        functools.partial(on_device, nlat, nlon),
        mesh=mesh,
        in_specs=(grid, rows, rows, P(), P(), grid),
        out_specs=(grid, grid, rows, rows),
        check_vma=False,
    )
```

time: 390 us -> 99.5 us (0.26); the launches traced: 385 us -> 99.2 us
  waiting for transfers between devices: 170 us -> 0 us
  Pallas kernels: 0 us -> 86.2 us
  local copies, waits for them, and re-layouts: 92.8 us -> 8.79 us
  matrix products: 52.7 us -> 0 us
  other arithmetic: 30.7 us -> 3.34 us
  starting transfers between devices: 15.6 us -> 0 us
  between operations: 14.9 us -> 0.95 us
  blocking collectives: 7.6 us -> 0 us
    psum x1 -> x0, waiting for transfers between devices: 92.3 us -> none  [on_device(): summed = lax.psum(shard_sum, 'lat').astype(jnp.float32)]
    pallas_call x0 -> x1, Pallas kernels: none -> 86.2 us  [on_device(): pl.pallas_call(functools.partial(kernel, nlat, nlon), out_shape=(jax.Shap...]
    dot_general x12 -> x0, matrix products: 52.7 us -> none  [the longest x1 18.4 us: on_device(): jnp.einsum('abhqk,abkhd->abqhd', dscore, key_u, preferred_element_type=jn...]
    reduce_scatter x1 -> x0, waiting for transfers between devices: 30.4 us -> none  [on_device(): lax.psum_scatter(jnp.concatenate([cross_rows(tok_part, grad_proj), cross_...]
    all_gather x1 -> x0, waiting for transfers between devices: 27.4 us -> none  [on_device(): lax.all_gather(w_qkv, 'lon', axis=0, tiled=True)]
    transpose x8 -> x0, local copies, waits for them, and re-layouts: 20.2 us -> none  [the longest x1 5.52 us: on_device(): jnp.einsum('abhqk,abqhd->abkhd', probs_b, grad_u, preferred_element_type=...]
    ppermute x8 -> x0, waiting for transfers between devices: 19.6 us -> none  [the longest x2 10.8 us: with_halo(): after = lax.ppermute(initial, axis, down)]
    slice x16 -> x25, local copies, waits for them, and re-layouts: 21.6 us -> 4.92 us  [the longest x4 3.78 us: quarters(): x = jnp.stack([x[l] for l in LEVELS])]
  transfers between devices with their start and end apart: 11 -> 0, of which waited for: 6 -> 0; matrix products, arithmetic and copies ran while one was open for 16% -> 0% of each run, Pallas kernels for 0% -> 0%
where the time goes in v1:
time: 99.5 us; the launch traced here: 99.2 us
  Pallas kernels  86.2 us (87%)
  local copies, waits for them, and re-layouts  8.79 us (9%)
  other arithmetic  3.34 us (3%)
    pallas_call x1, Pallas kernels, on_device(): pl.pallas_call(functools.partial(kernel, nlat, nlon), out_shape=(jax.Shap...  86.2 us
    slice x4, local copies, waits for them, and re-layouts, quarters(): x = jnp.stack([x[l] for l in LEVELS])  3.78 us
    unnamed x12, local copies, waits for them, and re-layouts  2.85 us

profile of v1, /device:TPU:1, one launch (start us, length us, event | category | flops | bytes accessed | tf_op | source)
XLA Modules:
  0.0 99.2 jit_solution(10138697039533095499)
XLA Ops:
  0.6 1.1 %slice.84 = bf16[2,6,12,512]{3,0,2,1:T(2,128)(2,1)S(1)} slice(bf16[4,6,12,512]{3,0,2,1:T(4,128)(2,1)} %param.6), slice={[1:3], [0:6], [0:12], [0:512]} | slice | bytes 294912 | tf_op jit(solution)/shard_map/slice | solution.py:355
  1.8 1.1 %slice.87 = bf16[2,6,12,512]{3,0,2,1:T(2,128)(2,1)S(1)} slice(bf16[4,6,12,512]{3,0,2,1:T(4,128)(2,1)} %param.11), slice={[1:3], [0:6], [0:12], [0:512]} | slice | bytes 294912 | tf_op jit(solution)/shard_map/slice | solution.py:355
  2.9 1.3 %fusion.3 = (bf16[1,6,12,512]{3,0,2,1:T(2,128)(2,1)S(1)}, bf16[1,6,12,512]{3,0,2,1:T(2,128)(2,1)S(1)}) fusion(bf16[4,6,12,512]{3,0,2,1:T(4,128)(2,1)} %param.6), kind=kLoop, calls=%fused_computation.12 | loop fusion | bytes 294912 | tf_op jit(solution)/shard_map/slice | solution.py:355
  4.2 0.5 pad_maximum_fusion.3
  4.7 0.2 copy.39
  5.0 0.1 reshape.40
  5.2 0.2 fusion.4
  5.4 0.5 pad_maximum_fusion.4
  5.9 0.2 copy.38
  6.2 0.1 reshape.42
  6.4 0.9 copy-done
  7.3 86.2 %shard_map.93 = (bf16[4,144,512]{2,1,0:T(8,128)(2,1)S(1)}, bf16[256,2048]{1,0:T(8,128)(2,1)S(1)}) custom-call(bf16[4,144,512]{2,1,0:T(8,128)(2,1)S(1)} %pad_maximum_fusion.x_ref, bf16[256,1536]{1,0:T(8,128)(2,1)S(1)} %copy-done, bf16[256,512]{1,0:T(8,128)(2,1)S(1)} %copy-done.1, f32[1,512]{1,0:T(1,128)S(1)} %bitcast.19, f32[8]{0:T(128)S(1)} %copy-done.3), custom_call_target="tpu_custom_call" | custom-call | tf_op jit(solution)/shard_map/pallas_call | solution.py:364
  93.5 0.2 copy.29
  93.7 0.1 reshape.45
  93.8 0.2 fusion.1
  94.3 0.1 pad_maximum_fusion.2
  94.4 0.9 copy.35
  95.3 0.2 copy.24
  95.5 0.1 reshape.44
  95.6 0.2 fusion.2
  96.1 0.1 pad_maximum_fusion.1
  96.1 0.9 copy.34
  97.1 0.8 slice_convert_fusion.1
  97.9 1.3 %slice_convert_fusion = f32[256,1536]{1,0:T(8,128)} fusion(bf16[256,2048]{1,0:T(8,128)(2,1)S(1)} %get-tuple-element.7), kind=kLoop, calls=%fused_computation | loop fusion | flops 393216 | bytes 2359296 | tf_op jit(solution)/shard_map/convert_element_type | solution.py:408
  (29 shorter events, 0.7 us)
Async XLA Ops:
  4.2 1.0 copy-start.4
  6.1 1.1 %copy-start = (bf16[256,1536]{1,0:T(8,128)(2,1)S(1)}, bf16[256,1536]{1,0:T(8,128)(2,1)}, u32[]{:S(2)}) copy-start(bf16[256,1536]{1,0:T(8,128)(2,1)} %wq_ref.1) | copy-start | bytes 2359300
  6.1 1.2 %copy-start.1 = (bf16[256,512]{1,0:T(8,128)(2,1)S(1)}, bf16[256,512]{1,0:T(8,128)(2,1)}, u32[]{:S(2)}) copy-start(bf16[256,512]{1,0:T(8,128)(2,1)} %wo_ref.1) | copy-start | bytes 786436
  6.2 1.2 %copy-start.2 = (f32[512]{0:T(512)S(1)}, f32[512]{0:T(512)}, u32[]{:S(2)}) copy-start(f32[512]{0:T(512)} %param.9) | copy-start | bytes 6148
  6.2 1.2 %copy-start.3 = (f32[8]{0:T(128)S(1)}, f32[8]{0:T(128)}, u32[]{:S(2)}) copy-start(f32[8]{0:T(128)} %tau_ref.1) | copy-start | bytes 100

commit v2 on v1

v2 whole, which is shorter than its diff:
```python
import functools

import jax
import jax.numpy as jnp
import numpy as np
from jax import lax
from jax.experimental import pallas as pl
from jax.experimental.pallas import tpu as pltpu
from jax.sharding import PartitionSpec as P

LV = 4
WH = 6
WW = 12
NORM_EPS = 1e-05
UNIT_EPS = 1e-06
MESH = pl.DeviceIdType.MESH
BF = jnp.bfloat16
F32 = jnp.float32
LEVELS = (0, 3, 1, 2)


def dot(a, b, ca, cb):
    return lax.dot_general(a, b, (((ca,), (cb,)), ((), ())), preferred_element_type=F32)


def bits_of(n):
    return n.bit_length() - 1


def norm_forward(y_rows):
    centered = y_rows - jnp.mean(y_rows, axis=-1, keepdims=True)
    inverse = lax.rsqrt(jnp.mean(centered * centered, axis=-1, keepdims=True) + NORM_EPS)
    return centered * inverse, inverse


def norm_back(normed, inverse, upstream):
    mean_up = jnp.mean(upstream, axis=-1, keepdims=True)
    mean_cross = jnp.mean(upstream * normed, axis=-1, keepdims=True)
    return inverse * (upstream - mean_up - normed * mean_cross)


class Copies:
    def __init__(self, send, recv):
        self.send, self.recv, self.used = send, recv, 0

    def make(self, src, dst, device):
        n = self.used
        self.used += 1
        return pltpu.make_async_remote_copy(
            src_ref=src, dst_ref=dst, send_sem=self.send.at[n], recv_sem=self.recv.at[n],
            device_id=device, device_id_type=MESH,
        )


def kernel(nlat, nlon, t_ref, c_ref, wq_ref, wo_ref, gain_ref, split_ref, window_ref, tau_ref,
           out_ref, gt_ref, g_ref,
           xs, xo, xq, w, tok, proj, qn, kn, probs, att, dy, da, dqkv, oq, oh,
           f0, f1, r0, r1, a0, a1, send, recv):
    lat, lon = lax.axis_index("lat"), lax.axis_index("lon")
    D = 512
    R = D // nlon
    H = R // 2
    H4 = R // 4
    xbit = (lat // 2) % 2
    core = lat % 2
    sibling = lat + 1 - 2 * core

    def flip(index, bit):
        v = (index // (1 << bit)) % 2
        return index + (1 - 2 * v) * (1 << bit), v

    def ahead(a, b):
        return ((lat + a) % nlat, (lon + b) % nlon)

    def behind(a, b):
        return ((lat + nlat - a) % nlat, (lon + nlon - b) % nlon)

    moves = ((0, 1), (1, 0), (1, 1))
    peers = [ahead(a, b) for a, b in moves] + [behind(a, b) for a, b in moves]
    core_group = [("lat", 0)]
    plane = [("lat", 1)] + [("lon", b) for b in reversed(range(bits_of(nlon)))]
    rest = [("lat", b) for b in range(2, bits_of(nlat))]
    strips = [("lat", 1)] + rest

    def member(group, k):
        at, place_mine, place_there = {"lat": lat, "lon": lon}, 0, 0
        for n, (axis, bit) in enumerate(group):
            there, mine = flip({"lat": lat, "lon": lon}[axis], bit)
            flipped = (k >> (len(group) - 1 - n)) & 1
            if flipped:
                at[axis] = at[axis] + (1 - 2 * mine) * (1 << bit)
            place_mine = 2 * place_mine + mine
            place_there = 2 * place_there + (1 - mine if flipped else mine)
        return (at["lat"], at["lon"]), place_mine, place_there

    for group in (core_group, plane, rest, strips):
        peers += [member(group, k)[0] for k in range(1, 1 << len(group))]
    barrier = pltpu.get_barrier_semaphore()
    for device in peers:
        pl.semaphore_signal(barrier, inc=1, device_id=device, device_id_type=MESH)
    pl.semaphore_wait(barrier, len(peers))

    copies = Copies(send, recv)
    waits = []

    mine4 = core * H + xbit * H4

    def w_source(p):
        if p < 3:
            return wq_ref.at[pl.ds(mine4, H4), pl.ds(p * D, D)]
        return wo_ref.at[pl.ds(mine4, H4), :]

    across, through, forward = [[], [], [], []], [], []

    def cross(p):
        for d in range(1, nlon):
            c = copies.make(w_source(p), w.at[p, pl.ds(lon * R + mine4, H4), :],
                            (lat, (lon + d) % nlon))
            c.start()
            across[p].append(c)

    for p in range(3):
        cross(p)

    xs[...] = jnp.zeros_like(xs)
    halo = []
    for kind, ref in enumerate((t_ref, c_ref)):
        for l in range(LV):
            for r in range(WH):
                first = (l * WH + r) * 16
                xs[kind, first:first + WW, :] = ref[l, r]
        xo[kind] = dot(split_ref[...], xs[kind], 1, 0).astype(BF).reshape(4, 80, D)
        halo.append([])
        for a, b in moves:
            c = copies.make(xo.at[kind, 2 * a + b], xq.at[kind, 2 * (1 - a) + 1 - b], ahead(a, b))
            c.start()
            halo[kind].append(c)
        xq[kind, 3] = xo[kind, 0]
    cross(3)

    for p in range(4):
        one, two = [], []
        for d in range(1, nlon):
            there = ((lon + nlon - d) % nlon) * R
            part = w.at[p, pl.ds(there + mine4, H4), :]
            one.append(copies.make(part, part, (flip(lat, 1)[0], lon)))
            part = w.at[p, pl.ds(there + core * H, H), :]
            two.append(copies.make(part, part, (sibling, lon)))
        through.append(one)
        forward.append(two)

    for p in range(3):
        w[p, pl.ds(lon * R, R), :] = wq_ref[:, p * D:(p + 1) * D]
    w[3, pl.ds(lon * R, R), :] = wo_ref[...]

    def windowed(kind):
        for c in halo[kind]:
            c.wait_recv()
        return dot(window_ref[...], xq[kind].reshape(320, D), 1, 0)

    def pass_on(before, after, p):
        for c in before[p]:
            c.wait_recv()
        for c in after[p]:
            c.start()

    def project(p):
        for c in forward[p]:
            c.wait_recv()
        proj[p] = dot(tok[...], w[p], 1, 0).astype(BF)

    for p in range(3):
        pass_on(across, through, p)
    tok[...] = windowed(0).astype(BF)
    for p in range(3):
        pass_on(through, forward, p)
        project(p)
    pass_on(across, through, 3)

    kk = lax.broadcasted_iota(jnp.int32, (144, 144), 0)
    qq = lax.broadcasted_iota(jnp.int32, (144, 144), 1)
    rows_ok = ((kk // 72) == (qq // 72)) | (jnp.zeros_like(kk) + lat != 0)
    level_ok = ((kk % 36) // 18) == ((qq % 36) // 18)

    def place(step):
        g, pair = step // 4, step % 4
        return (g, pair, pl.ds(pl.multiple_of(g * 144, 16), 144),
                pl.ds(pl.multiple_of(pair * 128, 128), 128))

    def halves(x):
        return x[:, :64], x[:, 64:]

    def unit(x):
        x = x.astype(F32)
        return (x * lax.rsqrt(jnp.sum(x * x, axis=-1, keepdims=True) + UNIT_EPS)).astype(BF)

    def forward_step(step, carry):
        g, pair, rs, cs = place(step)
        qs = [unit(x) for x in halves(proj[0, rs, cs])]
        ks = [unit(x) for x in halves(proj[1, rs, cs])]
        qn[rs, cs] = jnp.concatenate(qs, axis=1)
        kn[rs, cs] = jnp.concatenate(ks, axis=1)
        vs = halves(proj[2, rs, cs])
        mask = (rows_ok & (level_ok | (jnp.zeros_like(kk) + g == 1))).astype(F32)
        outs = []
        for i in range(2):
            s = dot(ks[i], qs[i], 1, 1) * tau_ref[2 * pair + i]
            e = jnp.exp(s) * mask
            p = e * (1.0 / jnp.sum(e, axis=0, keepdims=True))
            probs[2 * step + i] = p
            outs.append(dot(p.astype(BF), vs[i], 0, 0))
        att[rs, cs] = jnp.concatenate(outs, axis=1).astype(BF)
        return carry

    lax.fori_loop(0, 2, forward_step, 0)
    pass_on(through, forward, 3)
    lax.fori_loop(2, 8, forward_step, 0)
    cot = windowed(1)

    for c in forward[3]:
        c.wait_recv()
    normed, inverse = norm_forward(dot(att[...], w[3], 1, 0))
    gain = gain_ref[...]
    output = (tok[...].astype(F32) + gain * normed).astype(BF)
    homes = []

    def send_home(kind, value):
        oq[kind] = dot(window_ref[...], value, 0, 0).astype(BF).reshape(4, 80, D)
        for a, b in moves:
            c = copies.make(oq.at[kind, 2 * (1 - a) + 1 - b], oh.at[kind, 2 * a + b], behind(a, b))
            c.start()
            homes.append(c)
        oh[kind, 0] = oq[kind, 3]

    dy[...] = norm_back(normed, inverse, gain * cot).astype(BF)
    da[...] = dot(dy[...], w[3], 1, 1).astype(BF)

    def dv_step(step, carry):
        g, pair, rs, cs = place(step)
        das = halves(da[rs, cs])
        dqkv[2, rs, cs] = jnp.concatenate(
            [dot(probs[2 * step + i].astype(BF), das[i], 1, 0) for i in range(2)], axis=1
        ).astype(BF)
        return carry

    lax.fori_loop(0, 8, dv_step, 0)

    half = 4 * D

    def place_gradient(f, which, grad):
        for b in range(nlon):
            for ch in range(4):
                first = which * half + (ch // 2) * (half // 2) + b * 2 * R + (ch % 2) * R
                f[first:first + R, :] = grad[b * R:(b + 1) * R, ch * 128:(ch + 1) * 128]

    class Stream:
        def __init__(self, f, r, a):
            self.f, self.r, self.a = f, r, a
            self.size, self.off, self.base = 2 * half, 0, 0
            self.gsize, self.goff = 2 * half // nlon, 0
            self.done = []

        def start(self, group):
            n = 1 << len(group)
            self.size //= n
            self.now = []
            for k in range(1, n):
                device, _, there = member(group, k)
                give = pl.multiple_of(self.off + there * self.size, 16)
                c = copies.make(self.f.at[pl.ds(give, self.size), :],
                                self.r.at[pl.ds(self.base, self.size), :], device)
                c.start()
                self.now.append((c, self.base))
                self.base += self.size
            self.off = self.off + member(group, 0)[1] * self.size
            for axis, bit in group:
                if axis == "lat":
                    self.gsize //= 2
                    self.goff = self.goff + flip(lat, bit)[1] * self.gsize

        def finish(self, last=False):
            keep = pl.ds(pl.multiple_of(self.off, 16), self.size)
            total = self.f[keep, :].astype(F32)
            for c, base in self.now:
                c.wait_recv()
                total = total + self.r[base:base + self.size, :].astype(F32)
            self.done += [c for c, _ in self.now]
            if last:
                self.a[pl.ds(pl.multiple_of(self.goff, 16), self.size), :] = total.astype(BF)
            else:
                self.f[keep, :] = total.astype(BF)

        def gather(self, group, off, size):
            self.now = []
            part = self.a.at[pl.ds(pl.multiple_of(off, 16), size), :]
            for k in range(1, 1 << len(group)):
                c = copies.make(part, part, member(group, k)[0])
                c.start()
                self.now.append((c, 0))

        def gathered(self):
            for c, _ in self.now:
                c.wait_recv()
                self.done.append(c)

    s0 = Stream(f0, r0, a0)
    s1 = Stream(f1, r1, a1)
    half_rows = half // nlon

    place_gradient(f0, 0, dot(att[...], dy[...], 0, 0).astype(BF))
    place_gradient(f0, 1, dot(tok[...], dqkv[2], 0, 0).astype(BF))
    s0.start(core_group)
    send_home(0, output)

    def back(x, n, grad):
        x = x.astype(F32)
        scale = lax.rsqrt(jnp.sum(x * x, axis=-1, keepdims=True) + UNIT_EPS)
        inner = jnp.sum(x * grad, axis=-1, keepdims=True)
        return scale * (grad - x * (inner * scale * scale))

    def ds_step(step, carry):
        g, pair, rs, cs = place(step)
        das, vs = halves(da[rs, cs]), halves(proj[2, rs, cs])
        qs, ks = halves(proj[0, rs, cs]), halves(proj[1, rs, cs])
        qns, kns = halves(qn[rs, cs]), halves(kn[rs, cs])
        dqs, dks = [], []
        for i in range(2):
            p = probs[2 * step + i]
            dp = dot(vs[i], das[i], 1, 1)
            tot = jnp.sum(p * dp, axis=0, keepdims=True)
            ds = (tau_ref[2 * pair + i] * (p * (dp - tot))).astype(BF)
            dqs.append(back(qs[i], qns[i], dot(ds, kns[i], 0, 0)))
            dks.append(back(ks[i], kns[i], dot(ds, qns[i], 1, 0)))
        dqkv[0, rs, cs] = jnp.concatenate(dqs, axis=1).astype(BF)
        dqkv[1, rs, cs] = jnp.concatenate(dks, axis=1).astype(BF)
        return carry

    lax.fori_loop(0, 1, ds_step, 0)
    s0.finish()
    s0.start(plane)
    lax.fori_loop(1, 8, ds_step, 0)
    place_gradient(f1, 0, dot(tok[...], dqkv[0], 0, 0).astype(BF))
    place_gradient(f1, 1, dot(tok[...], dqkv[1], 0, 0).astype(BF))
    s1.start(core_group)
    s0.finish()
    s0.start(rest)
    s1.finish()
    s1.start(plane)

    grad_in = dot(dqkv[0], w[0], 1, 1) + dot(dqkv[1], w[1], 1, 1) + dot(dqkv[2], w[2], 1, 1)
    send_home(1, (cot + grad_in).astype(BF))
    s0.finish(True)
    s0.gather(strips, s0.goff, s0.gsize)
    s1.finish()
    s1.start(rest)
    s0.gathered()
    s0.gather(core_group, core * half_rows, half_rows)
    s1.finish(True)
    s1.gather(strips, s1.goff, s1.gsize)

    def bring(kind, ref):
        for c in homes[3 * kind:3 * kind + 3]:
            c.wait_recv()
        full = dot(split_ref[...], oh[kind].reshape(320, D), 0, 0).astype(BF)
        for l in range(LV):
            for r in range(WH):
                first = (l * WH + r) * 16
                ref[l, r] = full[first:first + WW, :]

    def collect(a, p, which):
        for ch in range(4):
            first = which * half_rows + ch * R
            g_ref[:, p * D + ch * 128:p * D + (ch + 1) * 128] = a[first:first + R, :]

    bring(0, out_ref)
    bring(1, gt_ref)
    s0.gathered()
    collect(a0, 3, 0)
    collect(a0, 2, 1)
    s1.gathered()
    s1.gather(core_group, core * half_rows, half_rows)
    s1.gathered()
    collect(a1, 0, 0)
    collect(a1, 1, 1)
    started = sum(halo + across + through + forward, []) + homes
    for c in started + s0.done + s1.done:
        c.wait_send()


def on_device(nlat, nlon, tokens, w_qkv, w_out, gain, tau, cotangent):
    D = tokens.shape[3]

    split = np.zeros((320, 384), np.float32)
    window = np.zeros((288, 320), np.float32)
    for q in range(4):
        for i in range(72):
            level, row, col = LEVELS[i // 18], 3 * (q // 2) + i % 18 // 6, 6 * (q % 2) + i % 6
            split[q * 80 + i, (level * WH + row) * 16 + col] = 1
            window[i // 36 * 144 + q * 36 + i % 36, q * 80 + i] = 1
    R = D // nlon
    half = 4 * D
    n_copies = 12 + 12 * (nlon - 1) + 2 * (2 * nlon - 1 + nlat // 4 - 1 + nlat // 2 - 1 + 2)
    vm = pl.BlockSpec(memory_space=pltpu.VMEM)
    output, grad_tokens, grads = pl.pallas_call(
        functools.partial(kernel, nlat, nlon),
        out_shape=(
            jax.ShapeDtypeStruct(tokens.shape, BF),
            jax.ShapeDtypeStruct(tokens.shape, BF),
            jax.ShapeDtypeStruct((R, 4 * D), BF),
        ),
        in_specs=[vm] * 7 + [pl.BlockSpec(memory_space=pltpu.SMEM)],
        out_specs=(vm, vm, vm),
        scratch_shapes=[
            pltpu.VMEM((2, 384, D), BF),
            pltpu.VMEM((2, 4, 80, D), BF),
            pltpu.VMEM((2, 4, 80, D), BF),
            pltpu.VMEM((4, D, D), BF),
            pltpu.VMEM((288, D), BF),
            pltpu.VMEM((3, 288, D), BF),
            pltpu.VMEM((288, D), BF),
            pltpu.VMEM((288, D), BF),
            pltpu.VMEM((16, 144, 144), F32),
            pltpu.VMEM((288, D), BF),
            pltpu.VMEM((288, D), BF),
            pltpu.VMEM((288, D), BF),
            pltpu.VMEM((3, 288, D), BF),
            pltpu.VMEM((2, 4, 80, D), BF),
            pltpu.VMEM((2, 4, 80, D), BF),
            pltpu.VMEM((2 * half, 128), BF),
            pltpu.VMEM((2 * half, 128), BF),
            pltpu.VMEM((2 * half, 128), BF),
            pltpu.VMEM((2 * half, 128), BF),
            pltpu.VMEM((2 * half // nlon, 128), BF),
            pltpu.VMEM((2 * half // nlon, 128), BF),
            pltpu.SemaphoreType.DMA((n_copies,)),
            pltpu.SemaphoreType.DMA((n_copies,)),
        ],
        compiler_params=pltpu.CompilerParams(
            collective_id=0, has_side_effects=True, vmem_limit_bytes=48 * 1024 * 1024
        ),
    )(tokens, cotangent, w_qkv, w_out, gain.reshape(1, D), jnp.asarray(split, BF),
      jnp.asarray(window, BF), tau)

    return (
        output,
        grad_tokens,
        grads[:, : 3 * D].astype(F32),
        grads[:, 3 * D :].astype(F32),
    )


def solution(mesh):
    nlat, nlon = mesh.shape["lat"], mesh.shape["lon"]
    grid = P(None, "lat", "lon", None)
    rows = P("lon", None)
    return jax.shard_map(
        functools.partial(on_device, nlat, nlon),
        mesh=mesh,
        in_specs=(grid, rows, rows, P(), P(), grid),
        out_specs=(grid, grid, rows, rows),
        check_vma=False,
    )
```

time: 99.5 us -> 86.6 us (0.87)
  Pallas kernels: 86.2 us -> 75.2 us
  other arithmetic: 3.34 us -> 2.16 us
    pallas_call x1, Pallas kernels: 86.2 us -> 75.2 us  [on_device(): pl.pallas_call(functools.partial(kernel, nlat, nlon), out_shape=(jax.Shap...]
    unnamed x12 -> x16, local copies, waits for them, and re-layouts: 2.85 us -> 8.19 us
    slice x25 -> x0, local copies, waits for them, and re-layouts: 4.92 us -> none  [the longest x4 3.78 us: quarters(): x = jnp.stack([x[l] for l in LEVELS])]
    another operation x4 -> x0, other arithmetic: 1.14 us -> none  [the longest x2 1 us: quarters(): x = jnp.stack([x[l] for l in LEVELS])]
    reshape x8 -> x0, local copies, waits for them, and re-layouts: 1.02 us -> none  [the longest x2 0.46 us: quarters(): x = x.reshape(LV, 2, WH // 2, 2, WW // 2, D).transpose(1, 3, 0, 2, 4, 5)]
where the time goes in v2:
time: 86.6 us; the launch traced here: 86.3 us
  Pallas kernels  75.2 us (87%)
  local copies, waits for them, and re-layouts  8.19 us (9%)
  other arithmetic  2.16 us (2%)
    pallas_call x1, Pallas kernels, on_device(): pl.pallas_call(functools.partial(kernel, nlat, nlon), out_shape=(jax.Shap...  75.2 us
    unnamed x16, local copies, waits for them, and re-layouts  8.19 us

profile of v2, /device:TPU:1, one launch (start us, length us, event | category | flops | bytes accessed | tf_op | source)
XLA Modules:
  0.0 86.3 jit_solution(13574522287805129918)
XLA Ops:
  0.6 0.0 copy-start
  0.6 1.1 %copy.12.t_ref = bf16[4,6,12,512]{3,2,1,0:T(8,128)(2,1)S(1)} copy(bf16[4,6,12,512]{3,0,2,1:T(4,128)(2,1)} %param.8) | data formatting | bytes 589824 | tf_op args[0]
  1.7 1.0 %copy.13.c_ref = bf16[4,6,12,512]{3,2,1,0:T(8,128)(2,1)S(1)} copy(bf16[4,6,12,512]{3,0,2,1:T(4,128)(2,1)} %param.13) | data formatting | bytes 589824 | tf_op args[5]
  2.8 0.0 copy-done
  2.8 0.0 copy-start.1
  2.8 0.9 %copy-done.1 = bf16[256,512]{1,0:T(8,128)(2,1)S(1)} copy-done((bf16[256,512]{1,0:T(8,128)(2,1)S(1)}, bf16[256,512]{1,0:T(8,128)(2,1)}, u32[]{:S(2)}) %copy-start.1) | copy-done | bytes 262168
  3.8 0.0 copy-start.2
  3.8 0.9 %copy-done.2 = bf16[320,384]{1,0:T(8,128)(2,1)S(1)} copy-done((bf16[320,384]{1,0:T(8,128)(2,1)S(1)}, bf16[320,384]{1,0:T(8,128)(2,1)}, u32[]{:S(2)}) %copy-start.2) | copy-done | bytes 245784
  4.7 0.0 copy-start.3
  4.7 0.9 %copy-done.3 = bf16[288,320]{1,0:T(8,128)(2,1)S(1)} copy-done((bf16[288,320]{1,0:T(8,128)(2,1)S(1)}, bf16[288,320]{1,0:T(8,128)(2,1)}, u32[]{:S(2)}) %copy-start.3) | copy-done | bytes 184344
  5.6 0.0 copy-start.4
  5.6 0.7 copy-done.4
  6.3 0.0 copy-start.5
  6.3 0.7 copy-done.5
  7.0 75.2 %shard_map.111 = (bf16[4,6,12,512]{3,2,1,0:T(8,128)(2,1)S(1)}, bf16[4,6,12,512]{3,2,1,0:T(8,128)(2,1)S(1)}, bf16[256,2048]{1,0:T(8,128)(2,1)S(1)}) custom-call(bf16[4,6,12,512]{3,2,1,0:T(8,128)(2,1)S(1)} %copy.12.t_ref, bf16[4,6,12,512]{3,2,1,0:T(8,128)(2,1)S(1)} %copy.13.c_ref, bf16[256,1536]{1,0:T(8,128)(2,1)S(1)} %copy-done, ...), custom_call_target="tpu_custom_call" | custom-call | tf_op jit(solution)/shard_map/pallas_call | solution.py:404
  82.2 0.9 %copy.14 = bf16[4,6,12,512]{3,0,2,1:T(4,128)(2,1)} copy(bf16[4,6,12,512]{3,2,1,0:T(8,128)(2,1)S(1)} %get-tuple-element.10) | data formatting | bytes 589824
  83.2 0.9 %copy.15 = bf16[4,6,12,512]{3,0,2,1:T(4,128)(2,1)} copy(bf16[4,6,12,512]{3,2,1,0:T(8,128)(2,1)S(1)} %get-tuple-element.11) | data formatting | bytes 589824
  84.1 0.8 slice_convert_fusion.1
  85.0 1.3 %slice_convert_fusion = f32[256,1536]{1,0:T(8,128)} fusion(bf16[256,2048]{1,0:T(8,128)(2,1)S(1)} %get-tuple-element.9), kind=kLoop, calls=%fused_computation | loop fusion | flops 393216 | bytes 2359296 | tf_op jit(solution)/shard_map/convert_element_type | solution.py:447
Async XLA Ops:
  0.6 2.2 %copy-start = (bf16[256,1536]{1,0:T(8,128)(2,1)S(1)}, bf16[256,1536]{1,0:T(8,128)(2,1)}, u32[]{:S(2)}) copy-start(bf16[256,1536]{1,0:T(8,128)(2,1)} %wq_ref.1) | copy-start | bytes 2359300
  2.8 1.0 %copy-start.1 = (bf16[256,512]{1,0:T(8,128)(2,1)S(1)}, bf16[256,512]{1,0:T(8,128)(2,1)}, u32[]{:S(2)}) copy-start(bf16[256,512]{1,0:T(8,128)(2,1)} %wo_ref.1) | copy-start | bytes 786436
  3.8 0.9 %copy-start.2 = (bf16[320,384]{1,0:T(8,128)(2,1)S(1)}, bf16[320,384]{1,0:T(8,128)(2,1)}, u32[]{:S(2)}) copy-start(bf16[320,384]{1,0:T(8,128)(2,1)} %constant.4.clone.split_ref) | copy-start | bytes 737284
  4.7 0.9 %copy-start.3 = (bf16[288,320]{1,0:T(8,128)(2,1)S(1)}, bf16[288,320]{1,0:T(8,128)(2,1)}, u32[]{:S(2)}) copy-start(bf16[288,320]{1,0:T(8,128)(2,1)} %constant.5.clone.window_ref) | copy-start | bytes 552964
  5.6 0.7 copy-start.4
  6.3 0.7 copy-start.5

commit v3 on v2

--- a/solution.py
+++ b/solution.py
@@ -52,9 +52,9 @@
         )
 
 
-def kernel(nlat, nlon, t_ref, c_ref, wq_ref, wo_ref, gain_ref, split_ref, window_ref, tau_ref,
+def kernel(nlat, nlon, t_hbm, c_hbm, wq_ref, wo_ref, gain_hbm, split_hbm, window_hbm, tau_ref,
            out_ref, gt_ref, g_ref,
-           xs, xo, xq, w, tok, proj, qn, kn, probs, att, dy, da, dqkv, oq, oh,
+           t_ref, c_ref, gain_ref, split_ref, window_ref, load, xs, xo, xq, w, tok, proj, qn, kn, probs, att, dy, da, dqkv, oq, oh,
            f0, f1, r0, r1, a0, a1, send, recv):
     lat, lon = lax.axis_index("lat"), lax.axis_index("lon")
     D = 512
@@ -74,6 +74,20 @@
 
     def behind(a, b):
         return ((lat + nlat - a) % nlat, (lon + nlon - b) % nlon)
+
+    loads = [
+        pltpu.make_async_copy(src, dst, load.at[n])
+        for n, (src, dst) in enumerate((
+            (t_hbm, t_ref), (c_hbm, c_ref), (split_hbm, split_ref),
+            (window_hbm, window_ref), (gain_hbm, gain_ref),
+            (wq_ref.at[:, pl.ds(0, D)], w.at[0, pl.ds(lon * R, R), :]),
+            (wq_ref.at[:, pl.ds(D, D)], w.at[1, pl.ds(lon * R, R), :]),
+            (wq_ref.at[:, pl.ds(2 * D, D)], w.at[2, pl.ds(lon * R, R), :]),
+            (wo_ref, w.at[3, pl.ds(lon * R, R), :]),
+        ))
+    ]
+    for c in loads:
+        c.start()
 
     moves = ((0, 1), (1, 0), (1, 1))
     peers = [ahead(a, b) for a, b in moves] + [behind(a, b) for a, b in moves]
@@ -123,13 +137,15 @@
         cross(p)
 
     xs[...] = jnp.zeros_like(xs)
+    for c in loads[:3]:
+        c.wait()
     halo = []
     for kind, ref in enumerate((t_ref, c_ref)):
-        for l in range(LV):
-            for r in range(WH):
-                first = (l * WH + r) * 16
-                xs[kind, first:first + WW, :] = ref[l, r]
-        xo[kind] = dot(split_ref[...], xs[kind], 1, 0).astype(BF).reshape(4, 80, D)
+        for r in range(WH):
+            for col in range(WW):
+                first = (r * WW + col) * 8
+                xs[kind, first:first + LV, :] = ref[r, col].astype(F32)
+        xo[kind] = dot(split_ref[...], xs[kind].astype(BF), 1, 0).astype(BF).reshape(4, 80, D)
         halo.append([])
         for a, b in moves:
             c = copies.make(xo.at[kind, 2 * a + b], xq.at[kind, 2 * (1 - a) + 1 - b], ahead(a, b))
@@ -149,9 +165,8 @@
         through.append(one)
         forward.append(two)
 
-    for p in range(3):
-        w[p, pl.ds(lon * R, R), :] = wq_ref[:, p * D:(p + 1) * D]
-    w[3, pl.ds(lon * R, R), :] = wo_ref[...]
+    for c in loads[3:]:
+        c.wait()
 
     def windowed(kind):
         for c in halo[kind]:
@@ -193,6 +208,12 @@
     def unit(x):
         x = x.astype(F32)
         return (x * lax.rsqrt(jnp.sum(x * x, axis=-1, keepdims=True) + UNIT_EPS)).astype(BF)
+
+    def twice(body):
+        def run(n, carry):
+            body(2 * n, carry)
+            return body(2 * n + 1, carry)
+        return run
 
     def forward_step(step, carry):
         g, pair, rs, cs = place(step)
@@ -212,9 +233,9 @@
         att[rs, cs] = jnp.concatenate(outs, axis=1).astype(BF)
         return carry
 
-    lax.fori_loop(0, 2, forward_step, 0)
+    lax.fori_loop(0, 1, twice(forward_step), 0)
     pass_on(through, forward, 3)
-    lax.fori_loop(2, 8, forward_step, 0)
+    lax.fori_loop(1, 4, twice(forward_step), 0)
     cot = windowed(1)
 
     for c in forward[3]:
@@ -243,7 +264,7 @@
         ).astype(BF)
         return carry
 
-    lax.fori_loop(0, 8, dv_step, 0)
+    lax.fori_loop(0, 4, twice(dv_step), 0)
 
     half = 4 * D
 
@@ -335,10 +356,10 @@
         dqkv[1, rs, cs] = jnp.concatenate(dks, axis=1).astype(BF)
         return carry
 
-    lax.fori_loop(0, 1, ds_step, 0)
+    lax.fori_loop(0, 1, twice(ds_step), 0)
     s0.finish()
     s0.start(plane)
-    lax.fori_loop(1, 8, ds_step, 0)
+    lax.fori_loop(1, 4, twice(ds_step), 0)
     place_gradient(f1, 0, dot(tok[...], dqkv[0], 0, 0).astype(BF))
     place_gradient(f1, 1, dot(tok[...], dqkv[1], 0, 0).astype(BF))
     s1.start(core_group)
@@ -361,11 +382,11 @@
     def bring(kind, ref):
         for c in homes[3 * kind:3 * kind + 3]:
             c.wait_recv()
-        full = dot(split_ref[...], oh[kind].reshape(320, D), 0, 0).astype(BF)
-        for l in range(LV):
-            for r in range(WH):
-                first = (l * WH + r) * 16
-                ref[l, r] = full[first:first + WW, :]
+        full = dot(split_ref[...], oh[kind].reshape(320, D), 0, 0)
+        for r in range(WH):
+            for col in range(WW):
+                first = (r * WW + col) * 8
+                ref[r, col] = full[first:first + LV, :].astype(BF)
 
     def collect(a, p, which):
         for ch in range(4):
@@ -390,12 +411,12 @@
 def on_device(nlat, nlon, tokens, w_qkv, w_out, gain, tau, cotangent):
     D = tokens.shape[3]
 
-    split = np.zeros((320, 384), np.float32)
+    split = np.zeros((320, 576), np.float32)
     window = np.zeros((288, 320), np.float32)
     for q in range(4):
         for i in range(72):
             level, row, col = LEVELS[i // 18], 3 * (q // 2) + i % 18 // 6, 6 * (q % 2) + i % 6
-            split[q * 80 + i, (level * WH + row) * 16 + col] = 1
+            split[q * 80 + i, (row * WW + col) * 8 + level] = 1
             window[i // 36 * 144 + q * 36 + i % 36, q * 80 + i] = 1
     R = D // nlon
     half = 4 * D
@@ -404,14 +425,20 @@
     output, grad_tokens, grads = pl.pallas_call(
         functools.partial(kernel, nlat, nlon),
         out_shape=(
-            jax.ShapeDtypeStruct(tokens.shape, BF),
-            jax.ShapeDtypeStruct(tokens.shape, BF),
+            jax.ShapeDtypeStruct((WH, WW, LV, D), BF),
+            jax.ShapeDtypeStruct((WH, WW, LV, D), BF),
             jax.ShapeDtypeStruct((R, 4 * D), BF),
         ),
-        in_specs=[vm] * 7 + [pl.BlockSpec(memory_space=pltpu.SMEM)],
+        in_specs=[pl.BlockSpec(memory_space=pl.ANY)] * 7 + [pl.BlockSpec(memory_space=pltpu.SMEM)],
         out_specs=(vm, vm, vm),
         scratch_shapes=[
-            pltpu.VMEM((2, 384, D), BF),
+            pltpu.VMEM((WH, WW, LV, D), BF),
+            pltpu.VMEM((WH, WW, LV, D), BF),
+            pltpu.VMEM((1, D), F32),
+            pltpu.VMEM(split.shape, BF),
+            pltpu.VMEM(window.shape, BF),
+            pltpu.SemaphoreType.DMA((9,)),
+            pltpu.VMEM((2, 576, D), F32),
             pltpu.VMEM((2, 4, 80, D), BF),
             pltpu.VMEM((2, 4, 80, D), BF),
             pltpu.VMEM((4, D, D), BF),
@@ -436,14 +463,14 @@
             pltpu.SemaphoreType.DMA((n_copies,)),
         ],
         compiler_params=pltpu.CompilerParams(
-            collective_id=0, has_side_effects=True, vmem_limit_bytes=48 * 1024 * 1024
+            collective_id=0, has_side_effects=True, vmem_limit_bytes=60 * 1024 * 1024
         ),
-    )(tokens, cotangent, w_qkv, w_out, gain.reshape(1, D), jnp.asarray(split, BF),
+    )(tokens.transpose(1, 2, 0, 3), cotangent.transpose(1, 2, 0, 3), w_qkv, w_out, gain.reshape(1, D), jnp.asarray(split, BF),
       jnp.asarray(window, BF), tau)
 
     return (
-        output,
-        grad_tokens,
+        output.transpose(2, 0, 1, 3),
+        grad_tokens.transpose(2, 0, 1, 3),
         grads[:, : 3 * D].astype(F32),
         grads[:, 3 * D :].astype(F32),
     )

time: 86.6 us -> 81.8 us (0.945)
  local copies, waits for them, and re-layouts: 8.19 us -> 1.44 us
  other arithmetic: 2.16 us -> 4.35 us
    unnamed x16 -> x6, local copies, waits for them, and re-layouts: 8.19 us -> 1.44 us
    convert_element_type x1, other arithmetic: 1.32 us -> 2.5 us  [on_device(): grads[:, :3 * D].astype(F32)]
    convert_element_type x1, other arithmetic: 0.84 us -> 1.85 us  [on_device(): grads[:, 3 * D:].astype(F32)]
where the time goes in v3:
time: 81.8 us; the launch traced here: 81.7 us
  Pallas kernels  75.2 us (92%)
  other arithmetic  4.35 us (5%)
  local copies, waits for them, and re-layouts  1.44 us (2%)
    pallas_call x1, Pallas kernels, on_device(): pl.pallas_call(functools.partial(kernel, nlat, nlon), out_shape=(jax.Shap...  75.2 us
    convert_element_type x1, other arithmetic, on_device(): grads[:, :3 * D].astype(F32)  2.5 us
    convert_element_type x1, other arithmetic, on_device(): grads[:, 3 * D:].astype(F32)  1.85 us

profile of v3, /device:TPU:1, one launch (start us, length us, event | category | flops | bytes accessed | tf_op | source)
XLA Modules:
  0.0 81.7 jit_solution(8013669889147001706)
XLA Ops:
  0.6 75.2 %shard_map.111 = (bf16[6,12,4,512]{3,2,1,0:T(4,128)(2,1)}, bf16[6,12,4,512]{3,2,1,0:T(4,128)(2,1)}, bf16[256,2048]{1,0:T(8,128)(2,1)}) custom-call(bf16[6,12,4,512]{3,2,1,0:T(4,128)(2,1)} %bitcast.7, bf16[6,12,4,512]{3,2,1,0:T(4,128)(2,1)} %bitcast.8, bf16[256,1536]{1,0:T(8,128)(2,1)} %wq_ref.1, bf16[256,512]{1,0:T(8,128)(2,1)} %wo_ref.1, f32[1,512]{1,0:T(1,128)} %bitcast.9, ...), custom_call_target="tpu_custom_call" | custom-call | tf_op jit(solution)/shard_map/pallas_call | solution.py:425
  75.9 0.0 copy-start.1
  75.9 1.8 %slice_convert_fusion.1 = f32[256,512]{1,0:T(8,128)} fusion(bf16[256,2048]{1,0:T(8,128)(2,1)} %get-tuple-element.9), kind=kLoop, calls=%fused_computation.1 | loop fusion | flops 131072 | bytes 786432 | tf_op jit(solution)/shard_map/convert_element_type | solution.py:475
  77.7 0.0 copy-start
  77.7 2.5 %slice_convert_fusion = f32[256,1536]{1,0:T(8,128)} fusion(bf16[256,2048]{1,0:T(8,128)(2,1)} %get-tuple-element.9), kind=kLoop, calls=%fused_computation | loop fusion | flops 393216 | bytes 2359296 | tf_op jit(solution)/shard_map/convert_element_type | solution.py:474
  80.2 0.0 copy-done.1
  80.2 0.7 copy.14
  80.9 0.0 copy-done
  80.9 0.7 copy.15
Async XLA Ops:
  75.9 4.4 %copy-start.1 = (bf16[6,12,4,512]{3,2,1,0:T(4,128)(2,1)S(1)}, bf16[6,12,4,512]{3,2,1,0:T(4,128)(2,1)}, u32[]{:S(2)}) copy-start(bf16[6,12,4,512]{3,2,1,0:T(4,128)(2,1)} %get-tuple-element.7) | copy-start | bytes 884740
  77.7 3.2 %copy-start = (bf16[6,12,4,512]{3,2,1,0:T(4,128)(2,1)S(1)}, bf16[6,12,4,512]{3,2,1,0:T(4,128)(2,1)}, u32[]{:S(2)}) copy-start(bf16[6,12,4,512]{3,2,1,0:T(4,128)(2,1)} %get-tuple-element.8) | copy-start | bytes 884740
